TPU v7x, 128 devices: a whole 4x4x4 slice. The times are simulated.
128 devices in a mesh: gx: 8 (over z, y_lo), gy: 16 (over y_hi, x, core).
Axes of the slice: x: 4, y: 4 (y_hi: 2, y_lo: 2; y = y_hi * 2 + y_lo), z: 4, core: 2. Of those that a mesh axis runs over, the one named last changes fastest.
Arguments:
- corpus: bfloat16 [262144, 1024], P(('gx', 'gy')), may hold values from -6 to 6
- rotation_first: bfloat16 [16, 1024, 1024], P('gy', 'gx'), may hold values from -0.1875 to 0.1875
- rotation_second: bfloat16 [8, 1024, 1024], P('gx', 'gy'), may hold values from -0.1875 to 0.1875
- cross_first: int32 [8, 16, 1024], P('gx', 'gy'), may hold values from 0 to 2047, as said below
- cross_second: int32 [8, 16, 1024], P('gx', 'gy'), may hold values from 0 to 2047, as said below
Outputs:
- partitioned: bfloat16 [262144, 1024], P(('gx', 'gy'))
Inputs may be any that keep to these rules, and one draw needn't show every extreme that they name: For every block, the 1024 entries of cross_first are distinct local row indices. For every block, the 1024 entries of cross_second are distinct local row indices.
All inputs are finite; a program needn't handle non-finite values.
Results may differ from a plain program's by a relative error of at most 0.0049.
Values may be sent and summed in bfloat16 or wider, within the bound.
A program may use at most 64 MiB of HBM per device.

v0:
```python
import jax
import jax.numpy as jnp
from jax import lax
from jax.sharding import PartitionSpec as P


def from_partner(block, axis, distance):
    count = lax.axis_size(axis)
    route = []
    for low in range(count):
        high = low | 1 << distance
        if high != low and high < count:
            route += [(low, high), (high, low)]
    return lax.ppermute(block, axis, route)


def add_rows(data, piece):
    return jnp.dot(data, piece[0], preferred_element_type=jnp.float32)


def rotate_first(data, rotation):
    empty = jnp.zeros((data.shape[0], rotation.shape[2]), jnp.float32)

    def accumulate(total, piece, start):
        return add_rows(data, piece)

    total = accumulate(empty, lax.all_gather(rotation, "gx", axis=1, tiled=True), jnp.int32(0))
    return total.astype(jnp.bfloat16)


def rotate_second(data, rotation):
    empty = jnp.zeros((data.shape[0], rotation.shape[2]), jnp.float32)

    def accumulate(total, piece, start):
        return add_rows(data, piece)

    total = accumulate(empty, lax.all_gather(rotation, "gy", axis=1, tiled=True), jnp.int32(0))
    return total.astype(jnp.bfloat16)


def cross_first_level(data, index):
    bit_pos = lax.axis_size("gx").bit_length() - 2
    outgoing = data[index]
    incoming = from_partner(outgoing, "gx", bit_pos)
    return data.at[index].set(incoming)


def cross_second_level(data, index):
    bit_pos = lax.axis_size("gy").bit_length() - 2
    outgoing = data[index]
    incoming = from_partner(outgoing, "gy", bit_pos)
    return data.at[index].set(incoming)


def on_device(corpus, rotation_first, rotation_second, cross_first, cross_second):
    first_index = cross_first.reshape(-1)
    second_index = cross_second.reshape(-1)
    level_one = rotate_first(corpus, rotation_first)
    moved_one = cross_first_level(level_one, first_index)
    level_two = rotate_second(moved_one, rotation_second)
    result = cross_second_level(level_two, second_index)
    return result


def solution(mesh):
    in_specs = (
        P(("gx", "gy"), None),
        P("gy", "gx", None),
        P("gx", "gy", None),
        P("gx", "gy", None),
        P("gx", "gy", None),
    )
    out_specs = P(("gx", "gy"), None)
    return jax.shard_map(
        on_device, mesh=mesh, in_specs=in_specs, out_specs=out_specs, check_vma=False
    )
```

profile of v0, /device:TPU:0, one launch (start us, length us, event | category | flops | bytes accessed | tf_op | source)
XLA Modules:
  0.0 223.9 jit_solution(12925382413116782894)
XLA Ops:
  6.5 0.0 all-gather.3.cloned.1.call-start
  6.5 0.7 all-gather.3.cloned.1.call-update
  7.3 0.0 all-gather.5.cloned.1.call-start
  7.3 0.7 all-gather.5.cloned.1.call-update
  8.0 0.7 compare_select_fusion.1
  8.7 55.1 %all-gather.3.cloned.1.call-done = bf16[1,1024,1024]{2,1,0:T(8,128)(2,1)} async-done(((bf16[1,128,1024]{2,1,0:T(8,128)(2,1)}), bf16[1,1024,1024]{2,1,0:T(8,128)(2,1)}) %all-gather.3.cloned.1.call-update) | async-done | bytes 2097168 | tf_op jit(solution)/shard_map/all_gather | solution.py:27
  63.8 9.3 %convolution_convert_fusion.1 = bf16[2048,1024]{1,0:T(8,128)(2,1)} fusion(bf16[2048,1024]{1,0:T(8,128)(2,1)} %param.5, bf16[1,1024,1024]{2,1,0:T(8,128)(2,1)} %all-gather.3.cloned.1.call-done), kind=kOutput, calls=%fused_computation.5 | convolution fusion | flops 4297064448 | bytes 10485760 | tf_op jit(solution)/shard_map/dot_general | solution.py:18
  73.2 0.0 copy-start
  73.2 8.8 %gather_fusion = bf16[1024,1024]{1,0:T(8,128)(2,1)} fusion(bf16[2048,1024]{1,0:T(8,128)(2,1)} %convolution_convert_fusion.1, s32[1024]{0:T(1024)S(1)} %broadcast_clamp_fusion.1), kind=kCustom, calls=%fused_computation | custom fusion | bytes 4198400 | tf_op jit(solution)/shard_map/gather | solution.py:43
  82.0 1.2 collective-permute-start
  83.1 0.0 copy-done
  83.1 47.7 %collective-permute-done = bf16[1024,1024]{1,0:T(8,128)(2,1)S(1)} collective-permute-done((bf16[1024,1024]{1,0:T(8,128)(2,1)}, bf16[1024,1024]{1,0:T(8,128)(2,1)S(1)}, u32[]{:S(2)}, u32[]{:S(2)}) %collective-permute-start) | collective-permute-done | bytes 2097184 | tf_op jit(solution)/shard_map/ppermute | solution.py:14
  130.8 10.1 %scatter_fusion = bf16[2048,1024]{1,0:T(8,128)(2,1)} fusion(bf16[2048,1024]{1,0:T(8,128)(2,1)} %convolution_convert_fusion.1, s32[1024]{0:T(1024)S(1)} %bitcast.17, bf16[1024,1024]{1,0:T(8,128)(2,1)S(1)} %collective-permute-done), kind=kCustom, calls=%fused_computation.2 | custom fusion | bytes 6295552 | tf_op jit(solution)/shard_map/scatter | solution.py:45
  140.9 0.0 all-gather.5.cloned.1.call-done
  140.9 9.4 %convolution_convert_fusion = bf16[2048,1024]{1,0:T(8,128)(2,1)} fusion(bf16[2048,1024]{1,0:T(8,128)(2,1)} %scatter_fusion, bf16[1,1024,1024]{2,1,0:T(8,128)(2,1)} %all-gather.5.cloned.1.call-done), kind=kOutput, calls=%fused_computation.4 | convolution fusion | flops 4297064448 | bytes 10485760 | tf_op jit(solution)/shard_map/dot_general | solution.py:18
  150.3 8.7 %gather_fusion.1 = bf16[1024,1024]{1,0:T(8,128)(2,1)} fusion(bf16[2048,1024]{1,0:T(8,128)(2,1)} %convolution_convert_fusion, s32[1024]{0:T(1024)S(1)} %broadcast_clamp_fusion), kind=kCustom, calls=%fused_computation.1 | custom fusion | bytes 4198400 | tf_op jit(solution)/shard_map/gather | solution.py:50
  159.0 2.7 %collective-permute-start.1 = (bf16[1024,1024]{1,0:T(8,128)(2,1)}, bf16[1024,1024]{1,0:T(8,128)(2,1)S(1)}, u32[]{:S(2)}, u32[]{:S(2)}) collective-permute-start(bf16[1024,1024]{1,0:T(8,128)(2,1)} %gather_fusion.1), channel_id=1, source_target_pairs={{0,8},{8,0},{1,9},{9,1},{2,10},{10,2},{3,11},{11,3},{4,12},{12,4},... | collective-permute-start | bytes 6291464 | tf_op jit(solution)/shard_map/ppermute | solution.py:14
  161.7 45.2 %collective-permute-done.1 = bf16[1024,1024]{1,0:T(8,128)(2,1)S(1)} collective-permute-done((bf16[1024,1024]{1,0:T(8,128)(2,1)}, bf16[1024,1024]{1,0:T(8,128)(2,1)S(1)}, u32[]{:S(2)}, u32[]{:S(2)}) %collective-permute-start.1) | collective-permute-done | bytes 2097184 | tf_op jit(solution)/shard_map/ppermute | solution.py:14
  206.9 10.2 %scatter_fusion.1 = bf16[2048,1024]{1,0:T(8,128)(2,1)} fusion(bf16[2048,1024]{1,0:T(8,128)(2,1)} %convolution_convert_fusion, s32[1024]{0:T(1024)S(1)} %bitcast.15, bf16[1024,1024]{1,0:T(8,128)(2,1)S(1)} %collective-permute-done.1), kind=kCustom, calls=%fused_computation.3 | custom fusion | bytes 6295552 | tf_op jit(solution)/shard_map/scatter | solution.py:52
  (3 shorter events, 0.0 us)
Async XLA Ops:
  6.5 57.3 %all-gather.3.cloned.1.call-start = ((), (), s32[]{:S(2)}) async-start(), calls=%async_computation | async-start | bytes 2359296 | tf_op jit(solution)/shard_map/all_gather | solution.py:27
  7.3 133.6 %all-gather.5.cloned.1.call-start = ((), (), s32[]{:S(2)}) async-start(), calls=%async_computation.1 | async-start | bytes 2228224 | tf_op jit(solution)/shard_map/all_gather | solution.py:37
  73.2 10.0 %copy-start = (s32[1,1,1024]{2,1,0:T(1,128)S(1)}, s32[1,1,1024]{2,1,0:T(1,128)}, u32[]{:S(2)}) copy-start(s32[1,1,1024]{2,1,0:T(1,128)} %param.9) | copy-start | bytes 12292
  82.0 48.8 %collective-permute-start = (bf16[1024,1024]{1,0:T(8,128)(2,1)}, bf16[1024,1024]{1,0:T(8,128)(2,1)S(1)}, u32[]{:S(2)}, u32[]{:S(2)}) collective-permute-start(bf16[1024,1024]{1,0:T(8,128)(2,1)} %gather_fusion), channel_id=1, source_target_pairs={{0,64},{64,0},{16,80},{80,16},{32,96},{96,32},{48,112},{112,48},{1... | collective-permute-start | bytes 6291464 | tf_op jit(solution)/shard_map/ppermute | solution.py:14
  159.0 47.9 %collective-permute-start.1 = (bf16[1024,1024]{1,0:T(8,128)(2,1)}, bf16[1024,1024]{1,0:T(8,128)(2,1)S(1)}, u32[]{:S(2)}, u32[]{:S(2)}) collective-permute-start(bf16[1024,1024]{1,0:T(8,128)(2,1)} %gather_fusion.1), channel_id=1, source_target_pairs={{0,8},{8,0},{1,9},{9,1},{2,10},{10,2},{3,11},{11,3},{4,12},{12,4},... | collective-permute-start | bytes 6291464 | tf_op jit(solution)/shard_map/ppermute | solution.py:14
Sparse Core Ops, SparseCore 0:
  9.0 54.7 all-gather.2
  66.3 47.4 all-gather.4
where the time goes:
time: 224 us
  waiting for transfers between devices  149 us (67%)
  local copies, waits for them, and re-layouts  37.7 us (17%)
  matrix products  18.7 us (8%)
  between operations  13.4 us (6%)
  starting transfers between devices  3.88 us (2%)
    ppermute x2, waiting for transfers between devices, from_partner(): return lax.ppermute(block, axis, route)  92.9 us
    all_gather x1, waiting for transfers between devices, rotate_first(): lax.all_gather(rotation, 'gx', axis=1, tiled=True)  55.1 us
    dot_general x2, matrix products, add_rows(): return jnp.dot(data, piece[0], preferred_element_type=jnp.float32)  18.7 us
    scatter x1, local copies, waits for them, and re-layouts, cross_second_level(): return data.at[index].set(incoming)  10.2 us
    scatter x1, local copies, waits for them, and re-layouts, cross_first_level(): return data.at[index].set(incoming)  10.1 us
    gather x1, local copies, waits for them, and re-layouts, cross_first_level(): outgoing = data[index]  8.8 us
    gather x1, local copies, waits for them, and re-layouts, cross_second_level(): outgoing = data[index]  8.72 us
  transfers between devices with their start and end apart: 4, of which 3 were waited for; matrix products, arithmetic and copies ran while one was open for 13% of the time, Pallas kernels for 0%

commit v1 on v0

v1 whole, which is shorter than its diff:
```python
import jax
import jax.numpy as jnp
from jax import lax
from jax.experimental import pallas as pl
from jax.experimental.pallas import tpu as pltpu
from jax.sharding import PartitionSpec as P

MESH = pl.DeviceIdType.MESH
F32, BF16 = jnp.float32, jnp.bfloat16

D = 1024
ROWS = 2048
HALF = 1024
CHUNK = 128
STEPS = HALF // CHUNK
FIRST = 128
SECOND = 64
KEEP = 64
N_FIRST, N_SECOND = 12, 15
BLOCK = 512

AT_SECOND = N_FIRST
AT_ONE = AT_SECOND + N_SECOND
AT_TWO = AT_ONE + STEPS
AT_RANK = AT_TWO + STEPS
FLOWS = AT_RANK + 1


def rows_at(start, size, unit=16):
    if isinstance(start, int):
        return pl.ds(start, size)
    return pl.ds(pl.multiple_of(start, unit), size)


def dot(a, b):
    return jnp.dot(a, b, preferred_element_type=F32)


def ones_where(mask):
    return jnp.where(mask, 1.0, 0.0)


def iota(shape, dim):
    return lax.broadcasted_iota(jnp.int32, shape, dim).astype(F32)


def to_column(row_ref, column_ref):
    same = iota((128, 128), 0) == iota((128, 128), 1)

    @pl.loop(0, HALF // 128)
    def _(b):
        piece = row_ref[0:1, pl.ds(pl.multiple_of(b * 128, 128), 128)]
        column = jnp.sum(jnp.where(same, piece, 0.0), axis=1, keepdims=True)
        column_ref[rows_at(b * 128, 128), :] = jnp.broadcast_to(column, (128, 128))


def over_rows(term):
    def step(b, total):
        return total + jnp.sum(term(b), axis=0, keepdims=True)

    return lax.fori_loop(0, HALF // 128, step, jnp.zeros((1, HALF), F32))


def kernel(
    x_hbm, r1_hbm, r2_hbm, i1_hbm, i2_hbm, out_hbm,
    x, r1, r2, i1, i2, sent1, recv1, held1, raw2, sent2, recv2, y, yr, z, acc,
    col1, col2, colk, colg, rows, rank_out, rank_in,
    send_sem, recv_sem, load_sem, out_sem,
):
    gx, gy = lax.axis_index("gx"), lax.axis_index("gy")
    pz, py = gx // 2, gx % 2
    half, px, pc = gy // 8, (gy // 2) % 4, gy % 2

    def on_z(step):
        return lax.rem(pz + step + 4, 4)

    def part(zz, yy):
        return (zz * 2 + yy) * FIRST

    z_up, z_down, z_far = ((on_z(s) * 2 + py, gy) for s in (1, -1, 2))
    y_near = (pz * 2 + 1 - py, gy)
    far_gy = lax.rem(gy + 8, 16)
    y_far = (gx, far_gy)
    others = [
        (gx, half * 8 + lax.rem(px + dx, 4) * 2 + lax.rem(pc + dc, 2))
        for dx in range(4)
        for dc in range(2)
        if dx or dc
    ]

    loads = [
        pltpu.make_async_copy(src, dst, load_sem.at[i])
        for i, (src, dst) in enumerate(
            (
                (i1_hbm, i1),
                (x_hbm, x),
                (i2_hbm, i2),
                (r1_hbm, r1.at[rows_at(gx * FIRST, FIRST)]),
                (r2_hbm, r2.at[rows_at(gy * SECOND, SECOND)]),
            )
        )
    ]
    for load in loads:
        load.start()

    barrier = pltpu.get_barrier_semaphore()
    partners = [z_up, z_down, z_far, y_near, y_far, *others]
    for partner in partners:
        pl.semaphore_signal(barrier, inc=1, device_id=partner, device_id_type=MESH)
    pl.semaphore_wait(barrier, len(partners))

    def flow(number, src, dst, target):
        return pltpu.make_async_remote_copy(
            src_ref=src,
            dst_ref=dst,
            send_sem=send_sem.at[number],
            recv_sem=recv_sem.at[number],
            device_id=target,
            device_id_type=MESH,
        )

    def first(number, zz, yy, low, size, target, src=None):
        there = r1.at[rows_at(part(zz, yy) + low, size)]
        return flow(number, there if src is None else src, there, target)

    rest = FIRST - KEEP
    f = [
        first(0, pz, py, 0, FIRST, z_up, r1_hbm),
        first(1, pz, py, 0, FIRST, z_down, r1_hbm),
        first(2, pz, py, 0, FIRST, y_near, r1_hbm),
        first(3, on_z(-1), py, 0, 64, z_up),
        first(4, on_z(-1), py, 0, KEEP, y_near),
        first(5, on_z(1), py, 64, 64, z_down),
        first(6, on_z(1), py, 0, KEEP, y_near),
        first(7, pz, 1 - py, KEEP, rest, z_up),
        first(8, pz, 1 - py, KEEP, rest, z_down),
        first(9, on_z(2), py, 0, KEEP, y_near),
        first(10, on_z(-1), 1 - py, KEEP, rest // 2, z_up),
        first(11, on_z(1), 1 - py, KEEP + rest // 2, rest // 2, z_down),
    ]

    def second(number, owner, target, src=None):
        there = r2.at[rows_at(owner * SECOND, SECOND)]
        return flow(AT_SECOND + number, there if src is None else src, there, target)

    s = [second(0, gy, y_far, r2_hbm)]
    s += [second(1 + n, gy, t, r2_hbm) for n, t in enumerate(others)]
    s += [second(8 + n, far_gy, t) for n, t in enumerate(others)]

    def one(c):
        at = rows_at(c * CHUNK, CHUNK)
        return flow(AT_ONE + c, sent1.at[at], recv1.at[at], z_far)

    def two(c):
        at = rows_at(c * CHUNK, CHUNK)
        return flow(AT_TWO + c, sent2.at[at], recv2.at[at], y_far)

    ranks = flow(AT_RANK, rank_out, rank_in, y_far)

    for n in (0, 1, 2):
        f[n].start()
    for n in range(8):
        s[n].start()

    loads[0].wait()
    rows[0:1, :] = i1[...].astype(F32)
    to_column(rows.at[0:1], col1)
    loads[1].wait()

    def pick_one(c):
        at = rows_at(c * CHUNK, CHUNK)
        hot = ones_where(col1[at, 0:1] == iota((CHUNK, ROWS), 1)).astype(BF16)
        sent1[at, :] = dot(hot, x[...]).astype(BF16)

    @pl.loop(0, 2)
    def _(c):
        pick_one(c)
        one(c).start()

    @pl.loop(2, STEPS)
    def _(c):
        pick_one(c)

    f[0].wait_recv()
    f[3].start()
    f[4].start()
    f[1].wait_recv()
    f[5].start()
    f[6].start()
    f[2].wait_recv()
    f[7].start()
    f[8].start()
    one(2).start()
    s[0].wait_recv()
    for n in range(8, 15):
        s[n].start()

    loads[2].wait()
    rows[1:2, :] = i2[...].astype(F32)
    to_column(rows.at[1:2], col2)
    held1[...] = jnp.zeros_like(held1)
    lane = iota((1, HALF), 1)

    def of_block(ref, b):
        return ref[rows_at(b * 128, 128), 0:1]

    own2 = rows[1:2, :]
    key = over_rows(
        lambda b: jnp.where(
            of_block(col1, b) == own2,
            iota((128, HALF), 0) + (b * 128 + 1).astype(F32),
            0.0,
        )
    )
    order = key * HALF + lane
    rows[2:3, :] = order
    to_column(rows.at[2:3], colk)
    rank = over_rows(lambda b: ones_where(of_block(colk, b) < order))
    rank_out[...] = jnp.broadcast_to(rank, rank_out.shape)
    ranks.start()

    f[3].wait_recv()
    f[9].start()
    f[7].wait_recv()
    f[10].start()
    f[8].wait_recv()
    f[11].start()
    for c in range(3, STEPS):
        one(c).start()

    source = jnp.where(key > 0.0, key + (ROWS - 1.0), own2)
    rows[3:4, :] = rank
    rows[4:5, :] = source

    @pl.loop(0, HALF // 128)
    def _(b):
        here = iota((128, HALF), 0) + (b * 128).astype(F32)
        found = jnp.where(rows[3:4, :] == here, rows[4:5, :], 0.0)
        colg[rows_at(b * 128, 128), :] = jnp.broadcast_to(
            jnp.sum(found, axis=1, keepdims=True), (128, 128)
        )

    @pl.loop(0, HALF // 256)
    def _(b):
        at = rows_at(b * 256, 256)
        hot = ones_where(colg[at, 0:1] == iota((256, ROWS), 1)).astype(BF16)
        raw2[at, :] = dot(hot, x[...]).astype(BF16)

    loads[3].wait()
    for n in (4, 5, 6, 9, 10, 11):
        f[n].wait_recv()

    def settle(p):
        at = rows_at(p * CHUNK, CHUNK)
        z[0:CHUNK, :] = dot(yr[at, :], r2[...]).astype(BF16)
        two(p).wait_recv()
        z[CHUNK : 2 * CHUNK, :] = dot(recv2[at, :], r2[...]).astype(BF16)
        lanes = pl.ds(pl.multiple_of(p * CHUNK, CHUNK), CHUNK)
        return jnp.concatenate([rows[5:6, lanes], rows[6:7, lanes]], axis=1)

    def place(to, t):
        at = rows_at(t * BLOCK, BLOCK)
        hit = to == iota((BLOCK, 2 * CHUNK), 0) + (t * BLOCK).astype(F32)
        hot = ones_where(hit)
        new = dot(hot.astype(BF16), z[...])
        old = acc[at, :].astype(F32)
        some = jnp.max(hot, axis=1, keepdims=True)
        acc[at, :] = jnp.where(some > 0.0, new, old).astype(BF16)

    def rotate(src, by, dst, low, high):
        @pl.loop(low, high)
        def _(t):
            at = rows_at(t * BLOCK, BLOCK)
            dst[at, :] = dot(src[at, :], by[...]).astype(BF16)

    @pl.loop(0, STEPS)
    def _(c):
        at = rows_at(c * CHUNK, CHUNK)
        one(c).wait_recv()
        held1[at, :] = recv1[at, :]
        hot = ones_where(colg[at, 0:1] - float(ROWS) == iota((CHUNK, HALF), 1))
        raw = raw2[at, :].astype(F32) + dot(hot.astype(BF16), held1[...])
        sent2[at, :] = dot(raw.astype(BF16), r1[...]).astype(BF16)
        two(c).start()
        yr[at, :] = dot(recv1[at, :], r1[...]).astype(BF16)

        @pl.when(c == 0)
        def _():
            rotate(x, r1, y, 0, 2)
            own1 = rows[0:1, :]
            taken = over_rows(lambda b: ones_where(of_block(col2, b) == own1))
            rows[5:6, :] = jnp.where(taken > 0.0, -1.0, own1)

        @pl.when(c == 1)
        def _():
            rotate(x, r1, y, 2, 4)
            ranks.wait_recv()
            rows[2:3, :] = rank_in[0:1, :]
            to_column(rows.at[2:3], colk)
            lanes = iota((128, HALF), 1)
            rows[6:7, :] = over_rows(
                lambda b: jnp.where(
                    of_block(colk, b) == lanes, of_block(col2, b), 0.0
                )
            )

        @pl.when(c == 2)
        def _():
            loads[4].wait()
            for n in range(1, 15):
                s[n].wait_recv()
            rotate(y, r2, acc, 0, 3)

        @pl.when(c == 3)
        def _():
            rotate(y, r2, acc, 3, 4)

        def since(k):
            return (c >= k).astype(jnp.int32)

        low = since(4) + 2 * since(5) + 2 * since(6) + since(7)
        high = since(3) + 2 * since(4) + 2 * since(5) + since(6) + since(7)

        @pl.loop(low, high)
        def _(p):
            to = settle(p)

            @pl.loop(0, ROWS // BLOCK)
            def _(t):
                place(to, t)

    def write(t):
        at = rows_at(t * BLOCK, BLOCK)
        return pltpu.make_async_copy(acc.at[at], out_hbm.at[at], out_sem.at[t])

    last = settle(STEPS - 1)

    @pl.loop(0, ROWS // BLOCK)
    def _(t):
        place(last, t)
        write(t).start()

    for n in range(N_FIRST):
        f[n].wait_send()
    for n in range(N_SECOND):
        s[n].wait_send()
    ranks.wait_send()
    for c in range(STEPS):
        one(c).wait_send()
        two(c).wait_send()
    for t in range(ROWS // BLOCK):
        write(t).wait()


def on_device(corpus, rotation_first, rotation_second, cross_first, cross_second):
    anywhere = pl.BlockSpec(memory_space=pl.ANY)
    return pl.pallas_call(
        kernel,
        out_shape=jax.ShapeDtypeStruct((ROWS, D), BF16),
        in_specs=[anywhere] * 5,
        out_specs=anywhere,
        scratch_shapes=[
            pltpu.VMEM((ROWS, D), BF16),
            pltpu.VMEM((D, D), BF16),
            pltpu.VMEM((D, D), BF16),
            pltpu.VMEM((1, HALF), jnp.int32),
            pltpu.VMEM((1, HALF), jnp.int32),
            pltpu.VMEM((HALF, D), BF16),
            pltpu.VMEM((HALF, D), BF16),
            pltpu.VMEM((HALF, D), BF16),
            pltpu.VMEM((HALF, D), BF16),
            pltpu.VMEM((HALF, D), BF16),
            pltpu.VMEM((HALF, D), BF16),
            pltpu.VMEM((ROWS, D), BF16),
            pltpu.VMEM((HALF, D), BF16),
            pltpu.VMEM((2 * CHUNK, D), BF16),
            pltpu.VMEM((ROWS, D), BF16),
            pltpu.VMEM((HALF, 128), F32),
            pltpu.VMEM((HALF, 128), F32),
            pltpu.VMEM((HALF, 128), F32),
            pltpu.VMEM((HALF, 128), F32),
            pltpu.VMEM((8, HALF), F32),
            pltpu.VMEM((8, HALF), F32),
            pltpu.VMEM((8, HALF), F32),
            pltpu.SemaphoreType.DMA((FLOWS,)),
            pltpu.SemaphoreType.DMA((FLOWS,)),
            pltpu.SemaphoreType.DMA((5,)),
            pltpu.SemaphoreType.DMA((ROWS // BLOCK,)),
        ],
        compiler_params=pltpu.CompilerParams(
            collective_id=0, has_side_effects=True, vmem_limit_bytes=48 << 20
        ),
        cost_estimate=pl.CostEstimate(
            flops=36 << 30, bytes_accessed=16 << 20, transcendentals=0
        ),
    )(
        corpus,
        rotation_first.reshape(FIRST, D),
        rotation_second.reshape(SECOND, D),
        cross_first.reshape(1, HALF),
        cross_second.reshape(1, HALF),
    )


def solution(mesh):
    in_specs = (
        P(("gx", "gy"), None),
        P("gy", "gx", None),
        P("gx", "gy", None),
        P("gx", "gy", None),
        P("gx", "gy", None),
    )
    out_specs = P(("gx", "gy"), None)
    return jax.shard_map(
        on_device, mesh=mesh, in_specs=in_specs, out_specs=out_specs, check_vma=False
    )
```

time: 224 us -> 126 us (0.56)
  waiting for transfers between devices: 149 us -> 0 us
  Pallas kernels: 0 us -> 120 us
  local copies, waits for them, and re-layouts: 37.7 us -> 5.24 us
  matrix products: 18.7 us -> 0 us
  between operations: 13.4 us -> 0.01 us
  starting transfers between devices: 3.88 us -> 0 us
    pallas_call x0 -> x1, Pallas kernels: none -> 120 us  [on_device(): pl.pallas_call(kernel, out_shape=jax.ShapeDtypeStruct((ROWS, D), BF16), i...]
    ppermute x2 -> x0, waiting for transfers between devices: 92.9 us -> none  [from_partner(): return lax.ppermute(block, axis, route)]
    all_gather x2 -> x0, waiting for transfers between devices: 55.1 us -> none  [the longest x1 55.1 us: rotate_first(): lax.all_gather(rotation, 'gx', axis=1, tiled=True)]
    scatter x2 -> x0, local copies, waits for them, and re-layouts: 20.2 us -> none  [the longest x1 10.2 us: cross_second_level(): return data.at[index].set(incoming)]
    dot_general x2 -> x0, matrix products: 18.7 us -> none  [add_rows(): return jnp.dot(data, piece[0], preferred_element_type=jnp.float32)]
    gather x2 -> x0, local copies, waits for them, and re-layouts: 17.5 us -> none  [the longest x1 8.8 us: cross_first_level(): outgoing = data[index]]
    unnamed x2 -> x9, local copies, waits for them, and re-layouts: 0.01 us -> 5.24 us
    ppermute x2 -> x0, starting transfers between devices: 3.84 us -> none  [from_partner(): return lax.ppermute(block, axis, route)]
  transfers between devices with their start and end apart: 4 -> 0, of which waited for: 3 -> 0; matrix products, arithmetic and copies ran while one was open for 13% -> 0% of each run, Pallas kernels for 0% -> 0%
where the time goes in v1:
time: 126 us; the launch traced here: 125 us
  Pallas kernels  120 us (95%)
  local copies, waits for them, and re-layouts  5.24 us (4%)
    pallas_call x1, Pallas kernels, on_device(): pl.pallas_call(kernel, out_shape=jax.ShapeDtypeStruct((ROWS, D), BF16), i...  120 us
    unnamed x9, local copies, waits for them, and re-layouts  5.24 us

profile of v1, /device:TPU:0, one launch (start us, length us, event | category | flops | bytes accessed | tf_op | source)
XLA Modules:
  0.0 125.5 jit_solution(17674813349604494315)
XLA Ops:
  0.0 0.0 copy-start
  0.0 0.9 copy-done
  1.0 0.0 copy-start.1
  1.0 0.9 copy-done.1
  1.9 0.0 copy-start.2
  1.9 0.7 copy-done.2
  2.5 0.0 copy-start.3
  2.5 0.7 copy-done.3
  3.2 120.2 %shard_map.55 = bf16[2048,1024]{1,0:T(8,128)(2,1)S(1)} custom-call(bf16[2048,1024]{1,0:T(8,128)(2,1)} %x_hbm.1, bf16[128,1024]{1,0:T(8,128)(2,1)S(1)} %bitcast.4, bf16[64,1024]{1,0:T(8,128)(2,1)S(1)} %bitcast.5, s32[1,1024]{1,0:T(1,128)S(1)} %bitcast.6, s32[1,1024]{1,0:T(1,128)S(1)} %bitcast.7), custom_call_target="tpu_custom_call" | custom-call | flops 38654705664 | bytes 16777216 | tf_op jit(solution)/shard_map/pallas_call | solution.py:357
  123.4 2.0 %copy.7 = bf16[2048,1024]{1,0:T(8,128)(2,1)} copy(bf16[2048,1024]{1,0:T(8,128)(2,1)S(1)} %shard_map.55) | data formatting | bytes 8388608
Async XLA Ops:
  0.0 0.9 copy-start
  1.0 0.9 copy-start.1
  1.9 0.7 copy-start.2
  2.5 0.7 copy-start.3

commit v2 on v1

v2 whole, which is shorter than its diff:
```python
import jax
import jax.numpy as jnp
from jax import lax
from jax.experimental import pallas as pl
from jax.experimental.pallas import tpu as pltpu
from jax.sharding import PartitionSpec as P

MESH = pl.DeviceIdType.MESH
F32, BF16 = jnp.float32, jnp.bfloat16

D = 1024
ROWS = 2048
HALF = 1024
CHUNK = 128
STEPS = HALF // CHUNK
FIRST = 128
SECOND = 64
N_FIRST, N_SECOND = 15, 15
BLOCK = 512
VMEM = 48 << 20
TAIL = 256

AT_SECOND = N_FIRST
AT_ONE = AT_SECOND + N_SECOND
AT_TWO = AT_ONE + STEPS + 1
AT_RANK = AT_TWO + STEPS + 1
FLOWS = AT_RANK + 1


def rows_at(start, size, unit=16):
    if isinstance(start, int):
        return pl.ds(start, size)
    return pl.ds(pl.multiple_of(start, unit), size)


def dot(a, b):
    return jnp.dot(a, b, preferred_element_type=F32)


def ones_where(mask):
    return jnp.where(mask, 1.0, 0.0)


def iota(shape, dim):
    return lax.broadcasted_iota(jnp.int32, shape, dim).astype(F32)


def to_column(row_ref, column_ref):
    same = iota((128, 128), 0) == iota((128, 128), 1)

    @pl.loop(0, HALF // 128)
    def _(b):
        piece = row_ref[0:1, pl.ds(pl.multiple_of(b * 128, 128), 128)]
        column = jnp.sum(jnp.where(same, piece, 0.0), axis=1, keepdims=True)
        column_ref[rows_at(b * 128, 128), :] = jnp.broadcast_to(column, (128, 128))


def over_rows(term):
    def step(b, total):
        return total + jnp.sum(term(b), axis=0, keepdims=True)

    return lax.fori_loop(0, HALF // 128, step, jnp.zeros((1, HALF), F32))


def kernel(
    x_hbm, r1_hbm, r2_hbm, i1_hbm, i2_hbm, acc, last_ref, to_ref,
    x, r1, r2, i1, i2, sent1, recv1, held1, raw2, sent2, y, late, z,
    col1, col2, colk, colg, keep, count, rows, to, rank_out, rank_in,
    send_sem, recv_sem, load_sem,
):
    gx, gy = lax.axis_index("gx"), lax.axis_index("gy")
    pz, py = gx // 2, gx % 2
    half, px, pc = gy // 8, (gy // 2) % 4, gy % 2

    def on_z(step):
        return lax.rem(pz + step + 4, 4)

    def part(zz, yy):
        return (zz * 2 + yy) * FIRST

    z_up, z_down, z_far = ((on_z(s) * 2 + py, gy) for s in (1, -1, 2))
    y_near = (pz * 2 + 1 - py, gy)
    far_gy = lax.rem(gy + 8, 16)
    y_far = (gx, far_gy)
    others = [
        (gx, half * 8 + lax.rem(px + dx, 4) * 2 + lax.rem(pc + dc, 2))
        for dx in range(4)
        for dc in range(2)
        if dx or dc
    ]

    loads = [
        pltpu.make_async_copy(src, dst, load_sem.at[i])
        for i, (src, dst) in enumerate(
            (
                (i1_hbm.at[0], i1),
                (i2_hbm.at[0], i2),
                (x_hbm, x),
                (r1_hbm.at[0], r1.at[rows_at(gx * FIRST, FIRST)]),
                (r2_hbm.at[0], r2.at[rows_at(gy * SECOND, SECOND)]),
            )
        )
    ]
    for load in loads:
        load.start()

    barrier = pltpu.get_barrier_semaphore()
    partners = [z_up, z_down, z_far, y_near, y_far, *others]
    for partner in partners:
        pl.semaphore_signal(barrier, inc=1, device_id=partner, device_id_type=MESH)
    pl.semaphore_wait(barrier, len(partners))

    def flow(number, src, dst, target):
        return pltpu.make_async_remote_copy(
            src_ref=src,
            dst_ref=dst,
            send_sem=send_sem.at[number],
            recv_sem=recv_sem.at[number],
            device_id=target,
            device_id_type=MESH,
        )

    def first(number, zz, yy, low, size, target, src=None):
        there = r1.at[rows_at(part(zz, yy) + low, size)]
        return flow(number, there if src is None else src, there, target)

    low, high = 0, FIRST // 2
    f = {
        "up_low": first(0, pz, py, low, 64, z_up, r1_hbm.at[0, 0:64]),
        "down_high": first(1, pz, py, high, 64, z_down, r1_hbm.at[0, 64:128]),
        "near_high": first(2, pz, py, high, 64, y_near, r1_hbm.at[0, 64:128]),
        "up_high": first(3, pz, py, high, 64, z_up, r1_hbm.at[0, 64:128]),
        "down_low": first(4, pz, py, low, 64, z_down, r1_hbm.at[0, 0:64]),
        "near_low": first(5, pz, py, low, 64, y_near, r1_hbm.at[0, 0:64]),
        "up_low_2": first(6, on_z(-1), py, low, 64, z_up),
        "down_high_2": first(7, on_z(1), py, high, 64, z_down),
        "near_up": first(8, on_z(-1), py, low, 64, y_near),
        "near_down": first(9, on_z(1), py, low, 64, y_near),
        "up_near": first(10, pz, 1 - py, high, 64, z_up),
        "down_near": first(11, pz, 1 - py, high, 64, z_down),
        "near_far": first(12, on_z(2), py, low, 64, y_near),
        "up_near_2": first(13, on_z(-1), 1 - py, high, 32, z_up),
        "down_near_2": first(14, on_z(1), 1 - py, high + 32, 32, z_down),
    }

    def forward(came, *names):
        f[came].wait_recv()
        for name in names:
            f[name].start()

    def second(number, owner, target, src=None):
        there = r2.at[rows_at(owner * SECOND, SECOND)]
        return flow(AT_SECOND + number, there if src is None else src, there, target)

    s = [second(0, gy, y_far, r2_hbm.at[0])]
    s += [second(1 + n, gy, t, r2_hbm.at[0]) for n, t in enumerate(others)]
    s += [second(8 + n, far_gy, t) for n, t in enumerate(others)]

    def one(c, at=0, size=CHUNK, number=None):
        rows_of = rows_at(c * CHUNK + at, size)
        number = c if number is None else number
        return flow(AT_ONE + number, sent1.at[rows_of], recv1.at[rows_of], z_far)

    def two(c, at=0, size=CHUNK, number=None):
        source = sent2.at[rows_at(c * CHUNK + at, size)]
        target = late.at[rows_at(c * 2 * CHUNK + CHUNK + at, size)]
        number = c if number is None else number
        return flow(AT_TWO + number, source, target, y_far)

    small = CHUNK // 2
    one_halves = [one(0, h * small, small, h * STEPS) for h in range(2)]
    two_halves = [two(0, h * small, small, h * STEPS) for h in range(2)]

    ranks = flow(AT_RANK, rank_out, rank_in, y_far)

    for name in list(f)[:6]:
        f[name].start()
    for n in range(1, 8):
        s[n].start()

    lane = iota((1, HALF), 1)

    def of_block(ref, b):
        return ref[rows_at(b * 128, 128), 0:1]

    loads[0].wait()
    rows[0:1, :] = i1[...].astype(F32)
    to_column(rows.at[0:1], col1)
    loads[1].wait()
    rows[1:2, :] = i2[...].astype(F32)
    own2 = rows[1:2, :]
    key = over_rows(
        lambda b: jnp.where(
            of_block(col1, b) == own2,
            iota((128, HALF), 0) + (b * 128 + 1).astype(F32),
            0.0,
        )
    )
    order = key * HALF + lane
    rows[2:3, :] = order
    rows[4:5, :] = jnp.where(key > 0.0, key + (ROWS - 1.0), own2)
    to_column(rows.at[2:3], colk)

    forward("up_low", "up_low_2", "near_up")
    forward("down_high", "down_high_2")
    forward("near_high", "up_near", "down_near")
    forward("down_low", "near_down")
    s[0].start()

    loads[2].wait()

    def pick_one(c):
        at = rows_at(c * 2 * CHUNK, 2 * CHUNK)
        hot = ones_where(col1[at, 0:1] == iota((2 * CHUNK, ROWS), 1)).astype(BF16)
        sent1[at, :] = dot(hot, x[...]).astype(BF16)

    pl.loop(0, STEPS // 2)(pick_one)

    forward("up_low_2", "near_far")
    forward("up_near", "up_near_2")
    forward("down_near", "down_near_2")
    s[0].wait_recv()
    for n in range(8, 15):
        s[n].start()

    order = rows[2:3, :]
    rank = over_rows(lambda b: ones_where(of_block(colk, b) < order))
    rank_out[...] = jnp.broadcast_to(rank, rank_out.shape)
    rows[3:4, :] = rank
    ranks.start()
    for name in ("up_high", "down_high_2", "up_near_2", "down_near_2"):
        f[name].wait_recv()
    for half_chunk in one_halves:
        half_chunk.start()
    for c in (1, 2):
        one(c).start()

    @pl.loop(0, HALF // 128)
    def _(b):
        here = iota((128, HALF), 0) + (b * 128).astype(F32)
        found = jnp.where(rows[3:4, :] == here, rows[4:5, :], 0.0)
        colg[rows_at(b * 128, 128), :] = jnp.broadcast_to(
            jnp.sum(found, axis=1, keepdims=True), (128, 128)
        )

    @pl.loop(0, HALF // 256)
    def _(b):
        at = rows_at(b * 256, 256)
        hot = ones_where(colg[at, 0:1] == iota((256, ROWS), 1)).astype(BF16)
        raw2[at, :] = dot(hot, x[...]).astype(BF16)

    held1[...] = jnp.zeros_like(held1)
    to_column(rows.at[1:2], col2)

    def table(ref, column):
        high = jnp.floor(ref * (1 / 128))
        low = column - jnp.floor(column * (1 / 128)) * 128
        hot_high = ones_where(high == iota((ROWS // 128, HALF), 0)).astype(BF16)
        hot_low = ones_where(low == iota((HALF, 128), 1)).astype(BF16)
        return dot(hot_high, hot_low)

    count[...] = table(rows[0:1, :], col1[...]) + table(rows[1:2, :], col2[...])
    same = iota((128, 128), 0) == iota((128, 128), 1)

    @pl.loop(0, ROWS // 128)
    def _(b):
        found = jnp.sum(
            jnp.where(same, count[pl.ds(b, 1), :], 0.0), axis=1, keepdims=True
        )
        column = jnp.where(found > 0.0, 0.0, 1.0)
        keep[rows_at(b * 128, 128), :] = jnp.broadcast_to(column, (128, 128))

    loads[3].wait()
    for name in ("near_low", "near_up", "near_down", "near_far"):
        f[name].wait_recv()

    def place(low, high):
        size = (high - low) * CHUNK
        source = z[low * CHUNK : high * CHUNK, :]
        target = to[0:1, low * CHUNK : high * CHUNK]

        def step(t):
            at = rows_at(t * BLOCK, BLOCK)
            hit = target == iota((BLOCK, size), 0) + (t * BLOCK).astype(F32)
            new = dot(ones_where(hit).astype(BF16), source)
            acc[at, :] = (acc[at, :].astype(F32) + new).astype(BF16)

        return step

    def rotate_block(src, by, dst, t, size=BLOCK):
        at = rows_at(t * size, size)
        dst[at, :] = dot(src[at, :], by[...]).astype(BF16)

    def settle_block(t):
        at = rows_at(t * BLOCK, BLOCK)
        kept = dot(y[at, :], r2[...]) * keep[at, 0:1]
        acc[at, :] = kept.astype(BF16)

    def rotate_came(t):
        came = dot(recv1[rows_at(t * 256, 256), :], r1[...]).astype(BF16)
        late[rows_at(t * 512, CHUNK), :] = came[0:CHUNK, :]
        late[rows_at(t * 512 + 2 * CHUNK, CHUNK), :] = came[CHUNK:, :]

    def pass_on(at):
        held1[at, :] = recv1[at, :]
        size = held1[at, :].shape[0]
        hot = ones_where(colg[at, 0:1] - float(ROWS) == iota((size, HALF), 1))
        raw = raw2[at, :].astype(F32) + dot(hot.astype(BF16), held1[...])
        sent2[at, :] = dot(raw.astype(BF16), r1[...]).astype(BF16)

    for h in range(2):
        one_halves[h].wait_recv()
        if h == 1:
            one(3).start()
        pass_on(pl.ds(h * small, small))
        two_halves[h].start()

    def spread(row, first):
        for p in range(STEPS):
            start = p * 2 * CHUNK + first
            to[0:1, start : start + CHUNK] = row[:, p * CHUNK : (p + 1) * CHUNK]

    def rest(c):
        def at_step(k):
            if isinstance(c, int):
                return lambda work: work() if c == k else None
            return pl.when(c == k) if k else lambda work: None

        @at_step(0)
        def _():
            pl.loop(0, 2)(lambda t: rotate_block(x, r1, y, t))
            own1 = rows[0:1, :]
            taken = over_rows(lambda b: ones_where(of_block(col2, b) == own1))
            spread(jnp.where(taken > 0.0, -1.0, own1), 0)

        @at_step(1)
        def _():
            pl.loop(2, 4)(lambda t: rotate_block(x, r1, y, t))
            ranks.wait_recv()
            rows[2:3, :] = rank_in[0:1, :]
            to_column(rows.at[2:3], colk)
            lanes = iota((128, HALF), 1)
            spread(
                over_rows(
                    lambda b: jnp.where(
                        of_block(colk, b) == lanes, of_block(col2, b), 0.0
                    )
                ),
                CHUNK,
            )

        @at_step(2)
        def _():
            loads[4].wait()
            for n in range(1, 15):
                s[n].wait_recv()
            pl.loop(0, 3)(settle_block)

        @at_step(3)
        def _():
            settle_block(jnp.int32(3))
            pl.loop(0, 2)(rotate_came)

        @at_step(4)
        def _():
            for half_chunk in two_halves:
                half_chunk.wait_recv()
            for n in (1, 2, 3):
                two(n).wait_recv()
            pl.loop(0, 2)(lambda t: rotate_block(late, r2, z, t))
            pl.loop(0, 1)(place(0, 8))

        @at_step(5)
        def _():
            pl.loop(1, 4)(place(0, 8))
            rotate_came(jnp.int32(2))

        @at_step(6)
        def _():
            for n in (4, 5):
                two(n).wait_recv()
            rotate_block(late, r2, z, jnp.int32(2))
            pl.loop(0, 4)(place(8, 12))

        @at_step(7)
        def _():
            rotate_came(jnp.int32(3))
            z[14 * CHUNK : 15 * CHUNK, :] = dot(
                late[14 * CHUNK : 15 * CHUNK, :], r2[...]
            ).astype(BF16)
            two(6).wait_recv()
            rotate_block(late, r2, z, jnp.int32(6), 256)
            pl.loop(0, 4)(place(12, 15))

    rest(0)

    @pl.loop(1, STEPS)
    def _(c):
        one(c).wait_recv()

        @pl.when(c < STEPS - 3)
        def _():
            one(c + 3).start()

        pass_on(rows_at(c * CHUNK, CHUNK))
        two(c).start()
        rest(c)

    to_ref[...] = jnp.broadcast_to(to[0:1, 15 * CHUNK :], to_ref.shape)
    two(STEPS - 1).wait_recv()
    last_ref[...] = dot(late[15 * CHUNK :, :], r2[...]).astype(BF16)

    for name in f:
        f[name].wait_send()
    for n in range(N_SECOND):
        s[n].wait_send()
    ranks.wait_send()
    for half_chunk in (*one_halves, *two_halves):
        half_chunk.wait_send()
    for c in range(1, STEPS):
        one(c).wait_send()
        two(c).wait_send()


def finish(acc, last, to, out_ref):
    start = pl.program_id(0) * TAIL
    hot = ones_where(to[0:1, :] == iota((TAIL, CHUNK), 0) + start.astype(F32))
    new = dot(hot.astype(BF16), last[...])
    old = acc[rows_at(start, TAIL), :].astype(F32)
    out_ref[...] = (old + new).astype(BF16)


def on_device(corpus, rotation_first, rotation_second, cross_first, cross_second):
    hbm = pl.BlockSpec(memory_space=pltpu.HBM)
    vmem = pl.BlockSpec(memory_space=pltpu.VMEM)
    acc, last, to = pl.pallas_call(
        kernel,
        out_shape=(
            jax.ShapeDtypeStruct((ROWS, D), BF16),
            jax.ShapeDtypeStruct((CHUNK, D), BF16),
            jax.ShapeDtypeStruct((8, CHUNK), F32),
        ),
        in_specs=[hbm] * 5,
        out_specs=(vmem, vmem, vmem),
        scratch_shapes=[
            pltpu.VMEM((ROWS, D), BF16),
            pltpu.VMEM((D, D), BF16),
            pltpu.VMEM((D, D), BF16),
            pltpu.VMEM((1, HALF), jnp.int32),
            pltpu.VMEM((1, HALF), jnp.int32),
            pltpu.VMEM((HALF, D), BF16),
            pltpu.VMEM((HALF, D), BF16),
            pltpu.VMEM((HALF, D), BF16),
            pltpu.VMEM((HALF, D), BF16),
            pltpu.VMEM((HALF, D), BF16),
            pltpu.VMEM((ROWS, D), BF16),
            pltpu.VMEM((ROWS, D), BF16),
            pltpu.VMEM((ROWS, D), BF16),
            pltpu.VMEM((HALF, 128), F32),
            pltpu.VMEM((HALF, 128), F32),
            pltpu.VMEM((HALF, 128), F32),
            pltpu.VMEM((HALF, 128), F32),
            pltpu.VMEM((ROWS, 128), F32),
            pltpu.VMEM((ROWS // 128, 128), F32),
            pltpu.VMEM((8, HALF), F32),
            pltpu.VMEM((8, ROWS), F32),
            pltpu.VMEM((8, HALF), F32),
            pltpu.VMEM((8, HALF), F32),
            pltpu.SemaphoreType.DMA((FLOWS,)),
            pltpu.SemaphoreType.DMA((FLOWS,)),
            pltpu.SemaphoreType.DMA((5,)),
        ],
        compiler_params=pltpu.CompilerParams(
            collective_id=0, has_side_effects=True, vmem_limit_bytes=VMEM
        ),
        cost_estimate=pl.CostEstimate(
            flops=36_000_000_000, bytes_accessed=16 << 20, transcendentals=0
        ),
    )(
        corpus,
        rotation_first,
        rotation_second,
        cross_first,
        cross_second,
    )
    return pl.pallas_call(
        finish,
        grid=(ROWS // TAIL,),
        out_shape=jax.ShapeDtypeStruct((ROWS, D), BF16),
        in_specs=[vmem] * 3,
        out_specs=pl.BlockSpec((TAIL, D), lambda t: (t, 0)),
        compiler_params=pltpu.CompilerParams(vmem_limit_bytes=12 << 20),
        cost_estimate=pl.CostEstimate(
            flops=600_000_000, bytes_accessed=8 << 20, transcendentals=0
        ),
    )(acc, last, to)


def solution(mesh):
    in_specs = (
        P(("gx", "gy"), None),
        P("gy", "gx", None),
        P("gx", "gy", None),
        P("gx", "gy", None),
        P("gx", "gy", None),
    )
    out_specs = P(("gx", "gy"), None)
    return jax.shard_map(
        on_device, mesh=mesh, in_specs=in_specs, out_specs=out_specs, check_vma=False
    )
```

time: 126 us -> 94.1 us (0.75)
  Pallas kernels: 120 us -> 90.6 us
  local copies, waits for them, and re-layouts: 5.24 us -> 3.23 us
    pallas_call x1 -> x2, Pallas kernels: 120 us -> 90.6 us  [the longest x1 86 us: on_device(): pl.pallas_call(kernel, out_shape=(jax.ShapeDtypeStruct((ROWS, D), BF16),...]
    unnamed x9 -> x8, local copies, waits for them, and re-layouts: 5.24 us -> 3.23 us
where the time goes in v2:
time: 94.1 us; the launch traced here: 93.9 us
  Pallas kernels  90.6 us (96%)
  local copies, waits for them, and re-layouts  3.23 us (3%)
    pallas_call x1, Pallas kernels, on_device(): pl.pallas_call(kernel, out_shape=(jax.ShapeDtypeStruct((ROWS, D), BF16),...  86 us
    pallas_call x1, Pallas kernels, on_device(): pl.pallas_call(finish, grid=(ROWS // TAIL,), out_shape=jax.ShapeDtypeStru...  4.63 us
    unnamed x8, local copies, waits for them, and re-layouts  3.23 us

profile of v2, /device:TPU:0, one launch (start us, length us, event | category | flops | bytes accessed | tf_op | source)
XLA Modules:
  0.0 93.9 jit_solution(10084325702999226223)
XLA Ops:
  0.0 0.0 copy-start
  0.0 0.9 %copy-done = bf16[1,128,1024]{2,1,0:T(8,128)(2,1)S(1)} copy-done((bf16[1,128,1024]{2,1,0:T(8,128)(2,1)S(1)}, bf16[1,128,1024]{2,1,0:T(8,128)(2,1)}, u32[]{:S(2)}) %copy-start) | copy-done | bytes 262168
  1.0 0.0 copy-start.1
  1.0 0.9 copy-done.1
  1.9 0.0 copy-start.2
  1.9 0.7 copy-done.2
  2.5 0.0 copy-start.3
  2.5 0.7 copy-done.3
  3.2 86.0 %shard_map.55 = (bf16[2048,1024]{1,0:T(8,128)(2,1)S(1)}, bf16[128,1024]{1,0:T(8,128)(2,1)S(1)}, f32[8,128]{1,0:T(8,128)S(1)}) custom-call(bf16[2048,1024]{1,0:T(8,128)(2,1)} %x_hbm.1, bf16[1,128,1024]{2,1,0:T(8,128)(2,1)S(1)} %copy-done, bf16[1,64,1024]{2,1,0:T(8,128)(2,1)S(1)} %copy-done.1, s32[1,1,1024]{2,1,0:T(1,128)S(1)} %copy-done.2, ...), custom_call_target="tpu_custom_call" | custom-call | flops 35999997952 | bytes 16777216 | tf_op jit(solution)/shard_map/pallas_call | solution.py:436
  89.2 4.6 %shard_map.56 = bf16[2048,1024]{1,0:T(8,128)(2,1)} custom-call(bf16[2048,1024]{1,0:T(8,128)(2,1)S(1)} %get-tuple-element.8.acc, bf16[128,1024]{1,0:T(8,128)(2,1)S(1)} %get-tuple-element.9.last, f32[8,128]{1,0:T(8,128)S(1)} %get-tuple-element.10.to), custom_call_target="tpu_custom_call" | custom-call | flops 600000000 | bytes 8388608 | tf_op jit(solution)/shard_map/pallas_call | solution.py:486
Async XLA Ops:
  0.0 0.9 %copy-start = (bf16[1,128,1024]{2,1,0:T(8,128)(2,1)S(1)}, bf16[1,128,1024]{2,1,0:T(8,128)(2,1)}, u32[]{:S(2)}) copy-start(bf16[1,128,1024]{2,1,0:T(8,128)(2,1)} %r1_hbm.1) | copy-start | bytes 786436
  1.0 0.9 copy-start.1
  1.9 0.7 copy-start.2
  2.5 0.7 copy-start.3

commit v3 on v2

--- a/solution.py
+++ b/solution.py
@@ -12,7 +12,9 @@
 ROWS = 2048
 HALF = 1024
 CHUNK = 128
-STEPS = HALF // CHUNK
+SMALL = 128
+STEPS = HALF // SMALL
+AHEAD = 3
 FIRST = 128
 SECOND = 64
 N_FIRST, N_SECOND = 15, 15
@@ -22,8 +24,8 @@
 
 AT_SECOND = N_FIRST
 AT_ONE = AT_SECOND + N_SECOND
-AT_TWO = AT_ONE + STEPS + 1
-AT_RANK = AT_TWO + STEPS + 1
+AT_TWO = AT_ONE + STEPS
+AT_RANK = AT_TWO + STEPS
 FLOWS = AT_RANK + 1
 
 
@@ -156,20 +158,16 @@
     s += [second(1 + n, gy, t, r2_hbm.at[0]) for n, t in enumerate(others)]
     s += [second(8 + n, far_gy, t) for n, t in enumerate(others)]
 
-    def one(c, at=0, size=CHUNK, number=None):
-        rows_of = rows_at(c * CHUNK + at, size)
-        number = c if number is None else number
-        return flow(AT_ONE + number, sent1.at[rows_of], recv1.at[rows_of], z_far)
-
-    def two(c, at=0, size=CHUNK, number=None):
-        source = sent2.at[rows_at(c * CHUNK + at, size)]
-        target = late.at[rows_at(c * 2 * CHUNK + CHUNK + at, size)]
-        number = c if number is None else number
-        return flow(AT_TWO + number, source, target, y_far)
-
-    small = CHUNK // 2
-    one_halves = [one(0, h * small, small, h * STEPS) for h in range(2)]
-    two_halves = [two(0, h * small, small, h * STEPS) for h in range(2)]
+    def late_at(c):
+        return c * 2 * CHUNK
+
+    def one(c):
+        at = rows_at(c * SMALL, SMALL)
+        return flow(AT_ONE + c, sent1.at[at], recv1.at[at], z_far)
+
+    def two(c):
+        target = late.at[rows_at(late_at(c) + CHUNK, SMALL)]
+        return flow(AT_TWO + c, sent2.at[rows_at(c * SMALL, SMALL)], target, y_far)
 
     ranks = flow(AT_RANK, rank_out, rank_in, y_far)
 
@@ -186,6 +184,7 @@
     loads[0].wait()
     rows[0:1, :] = i1[...].astype(F32)
     to_column(rows.at[0:1], col1)
+    held1[...] = jnp.zeros_like(held1)
     loads[1].wait()
     rows[1:2, :] = i2[...].astype(F32)
     own2 = rows[1:2, :]
@@ -207,33 +206,11 @@
     forward("down_low", "near_down")
     s[0].start()
 
-    loads[2].wait()
-
-    def pick_one(c):
-        at = rows_at(c * 2 * CHUNK, 2 * CHUNK)
-        hot = ones_where(col1[at, 0:1] == iota((2 * CHUNK, ROWS), 1)).astype(BF16)
-        sent1[at, :] = dot(hot, x[...]).astype(BF16)
-
-    pl.loop(0, STEPS // 2)(pick_one)
-
-    forward("up_low_2", "near_far")
-    forward("up_near", "up_near_2")
-    forward("down_near", "down_near_2")
-    s[0].wait_recv()
-    for n in range(8, 15):
-        s[n].start()
-
     order = rows[2:3, :]
     rank = over_rows(lambda b: ones_where(of_block(colk, b) < order))
     rank_out[...] = jnp.broadcast_to(rank, rank_out.shape)
     rows[3:4, :] = rank
     ranks.start()
-    for name in ("up_high", "down_high_2", "up_near_2", "down_near_2"):
-        f[name].wait_recv()
-    for half_chunk in one_halves:
-        half_chunk.start()
-    for c in (1, 2):
-        one(c).start()
 
     @pl.loop(0, HALF // 128)
     def _(b):
@@ -243,14 +220,27 @@
             jnp.sum(found, axis=1, keepdims=True), (128, 128)
         )
 
-    @pl.loop(0, HALF // 256)
-    def _(b):
-        at = rows_at(b * 256, 256)
-        hot = ones_where(colg[at, 0:1] == iota((256, ROWS), 1)).astype(BF16)
-        raw2[at, :] = dot(hot, x[...]).astype(BF16)
-
-    held1[...] = jnp.zeros_like(held1)
-    to_column(rows.at[1:2], col2)
+    def spread(row, first):
+        for p in range(HALF // CHUNK):
+            start = p * 2 * CHUNK + first
+            to[0:1, start : start + CHUNK] = row[:, p * CHUNK : (p + 1) * CHUNK]
+
+    def find_first():
+        own1 = rows[0:1, :]
+        taken = over_rows(lambda b: ones_where(of_block(col2, b) == own1))
+        spread(jnp.where(taken > 0.0, -1.0, own1), 0)
+
+    def find_second():
+        ranks.wait_recv()
+        rows[2:3, :] = rank_in[0:1, :]
+        to_column(rows.at[2:3], colk)
+        lanes = iota((128, HALF), 1)
+        spread(
+            over_rows(
+                lambda b: jnp.where(of_block(colk, b) == lanes, of_block(col2, b), 0.0)
+            ),
+            CHUNK,
+        )
 
     def table(ref, column):
         high = jnp.floor(ref * (1 / 128))
@@ -259,22 +249,54 @@
         hot_low = ones_where(low == iota((HALF, 128), 1)).astype(BF16)
         return dot(hot_high, hot_low)
 
-    count[...] = table(rows[0:1, :], col1[...]) + table(rows[1:2, :], col2[...])
-    same = iota((128, 128), 0) == iota((128, 128), 1)
-
-    @pl.loop(0, ROWS // 128)
-    def _(b):
-        found = jnp.sum(
-            jnp.where(same, count[pl.ds(b, 1), :], 0.0), axis=1, keepdims=True
-        )
-        column = jnp.where(found > 0.0, 0.0, 1.0)
-        keep[rows_at(b * 128, 128), :] = jnp.broadcast_to(column, (128, 128))
+    def find_kept():
+        count[...] = table(rows[0:1, :], col1[...]) + table(rows[1:2, :], col2[...])
+        same = iota((128, 128), 0) == iota((128, 128), 1)
+
+        @pl.loop(0, ROWS // 128)
+        def _(b):
+            found = jnp.sum(
+                jnp.where(same, count[pl.ds(b, 1), :], 0.0), axis=1, keepdims=True
+            )
+            column = jnp.where(found > 0.0, 0.0, 1.0)
+            keep[rows_at(b * 128, 128), :] = jnp.broadcast_to(column, (128, 128))
+
+    loads[2].wait()
+
+    def pick(column, dst, b):
+        at = rows_at(b * 256, 256)
+        hot = ones_where(column[at, 0:1] == iota((256, ROWS), 1)).astype(BF16)
+        dst[at, :] = dot(hot, x[...]).astype(BF16)
+
+    pick(col1, sent1, 0)
+    pl.loop(0, 1)(lambda b: pick(colg, raw2, b))
+    forward("up_low_2", "near_far")
+    forward("up_near", "up_near_2")
+    forward("down_near", "down_near_2")
+    s[0].wait_recv()
+    for n in range(8, 15):
+        s[n].start()
+    for name in ("up_high", "down_high_2", "up_near_2", "down_near_2"):
+        f[name].wait_recv()
+    for c in range(2):
+        one(c).start()
+    pick(col1, sent1, 1)
+    one(2).start()
+    pl.loop(1, 4)(lambda b: pick(colg, raw2, b))
+    to_column(rows.at[1:2], col2)
+    find_first()
 
     loads[3].wait()
     for name in ("near_low", "near_up", "near_down", "near_far"):
         f[name].wait_recv()
 
-    def place(low, high):
+    def prepare(b):
+        at = rows_at(b * 256, 256)
+        raw2[at, :] = dot(raw2[at, :], r1[...]).astype(BF16)
+
+    prepare(0)
+
+    def place(low, high, begin=False):
         size = (high - low) * CHUNK
         source = z[low * CHUNK : high * CHUNK, :]
         target = to[0:1, low * CHUNK : high * CHUNK]
@@ -283,7 +305,12 @@
             at = rows_at(t * BLOCK, BLOCK)
             hit = target == iota((BLOCK, size), 0) + (t * BLOCK).astype(F32)
             new = dot(ones_where(hit).astype(BF16), source)
-            acc[at, :] = (acc[at, :].astype(F32) + new).astype(BF16)
+            if begin:
+                old = dot(y[at, :], r2[...]) * keep[at, 0:1]
+                old = old.astype(BF16).astype(F32)
+            else:
+                old = acc[at, :].astype(F32)
+            acc[at, :] = (old + new).astype(BF16)
 
         return step
 
@@ -291,123 +318,101 @@
         at = rows_at(t * size, size)
         dst[at, :] = dot(src[at, :], by[...]).astype(BF16)
 
-    def settle_block(t):
-        at = rows_at(t * BLOCK, BLOCK)
-        kept = dot(y[at, :], r2[...]) * keep[at, 0:1]
-        acc[at, :] = kept.astype(BF16)
-
-    def rotate_came(t):
-        came = dot(recv1[rows_at(t * 256, 256), :], r1[...]).astype(BF16)
-        late[rows_at(t * 512, CHUNK), :] = came[0:CHUNK, :]
-        late[rows_at(t * 512 + 2 * CHUNK, CHUNK), :] = came[CHUNK:, :]
-
-    def pass_on(at):
-        held1[at, :] = recv1[at, :]
-        size = held1[at, :].shape[0]
-        hot = ones_where(colg[at, 0:1] - float(ROWS) == iota((size, HALF), 1))
-        raw = raw2[at, :].astype(F32) + dot(hot.astype(BF16), held1[...])
-        sent2[at, :] = dot(raw.astype(BF16), r1[...]).astype(BF16)
-
-    for h in range(2):
-        one_halves[h].wait_recv()
-        if h == 1:
-            one(3).start()
-        pass_on(pl.ds(h * small, small))
-        two_halves[h].start()
-
-    def spread(row, first):
-        for p in range(STEPS):
-            start = p * 2 * CHUNK + first
-            to[0:1, start : start + CHUNK] = row[:, p * CHUNK : (p + 1) * CHUNK]
+    def pass_on(c):
+        at = rows_at(c * SMALL, SMALL)
+        came = dot(recv1[at, :], r1[...]).astype(BF16)
+        held1[at, :] = came
+        late[rows_at(late_at(c), SMALL), :] = came
+
+        def choose(depth):
+            hot = ones_where(colg[at, 0:1] - float(ROWS) == iota((SMALL, depth), 1))
+            new = dot(hot.astype(BF16), held1[0:depth, :])
+            sent2[at, :] = (raw2[at, :].astype(F32) + new).astype(BF16)
+
+        low = 0
+        for depth in (256, 512, HALF):
+
+            @pl.when((c * SMALL >= low) & (c * SMALL < depth))
+            def _():
+                choose(depth)
+
+            low = depth
+
+    def rotated(low, high):
+        for n in range(low, high):
+            two(n).wait_recv()
 
     def rest(c):
         def at_step(k):
-            if isinstance(c, int):
-                return lambda work: work() if c == k else None
-            return pl.when(c == k) if k else lambda work: None
+            return pl.when(c == k)
+
+        def pairs(low, high):
+            rotated(low, high)
+            pl.loop(low, high)(lambda t: rotate_block(late, r2, z, t, 256))
 
         @at_step(0)
         def _():
+            pl.loop(2, 3)(lambda b: pick(col1, sent1, b))
             pl.loop(0, 2)(lambda t: rotate_block(x, r1, y, t))
-            own1 = rows[0:1, :]
-            taken = over_rows(lambda b: ones_where(of_block(col2, b) == own1))
-            spread(jnp.where(taken > 0.0, -1.0, own1), 0)
+            pl.loop(1, 2)(prepare)
 
         @at_step(1)
         def _():
+            find_kept()
             pl.loop(2, 4)(lambda t: rotate_block(x, r1, y, t))
-            ranks.wait_recv()
-            rows[2:3, :] = rank_in[0:1, :]
-            to_column(rows.at[2:3], colk)
-            lanes = iota((128, HALF), 1)
-            spread(
-                over_rows(
-                    lambda b: jnp.where(
-                        of_block(colk, b) == lanes, of_block(col2, b), 0.0
-                    )
-                ),
-                CHUNK,
-            )
 
         @at_step(2)
+        def _():
+            pl.loop(3, 4)(lambda b: pick(col1, sent1, b))
+            pl.loop(2, 4)(prepare)
+            find_second()
+
+        @at_step(3)
         def _():
             loads[4].wait()
             for n in range(1, 15):
                 s[n].wait_recv()
-            pl.loop(0, 3)(settle_block)
-
-        @at_step(3)
-        def _():
-            settle_block(jnp.int32(3))
-            pl.loop(0, 2)(rotate_came)
+            pairs(0, 2)
+            pl.loop(0, 1)(place(0, 4, True))
 
         @at_step(4)
         def _():
-            for half_chunk in two_halves:
-                half_chunk.wait_recv()
-            for n in (1, 2, 3):
-                two(n).wait_recv()
-            pl.loop(0, 2)(lambda t: rotate_block(late, r2, z, t))
-            pl.loop(0, 1)(place(0, 8))
+            pl.loop(1, 3)(place(0, 4, True))
 
         @at_step(5)
         def _():
-            pl.loop(1, 4)(place(0, 8))
-            rotate_came(jnp.int32(2))
+            pl.loop(3, 4)(place(0, 4, True))
+            pairs(2, 4)
+            pl.loop(0, 1)(place(4, 8))
 
         @at_step(6)
         def _():
-            for n in (4, 5):
-                two(n).wait_recv()
-            rotate_block(late, r2, z, jnp.int32(2))
-            pl.loop(0, 4)(place(8, 12))
+            pl.loop(1, 4)(place(4, 8))
+            pairs(4, 5)
+            pl.loop(0, 4)(place(8, 10))
 
         @at_step(7)
         def _():
-            rotate_came(jnp.int32(3))
             z[14 * CHUNK : 15 * CHUNK, :] = dot(
                 late[14 * CHUNK : 15 * CHUNK, :], r2[...]
             ).astype(BF16)
-            two(6).wait_recv()
-            rotate_block(late, r2, z, jnp.int32(6), 256)
-            pl.loop(0, 4)(place(12, 15))
-
-    rest(0)
-
-    @pl.loop(1, STEPS)
+            pairs(5, 7)
+            pl.loop(0, 4)(place(10, 15))
+
+    @pl.loop(0, STEPS)
     def _(c):
         one(c).wait_recv()
 
-        @pl.when(c < STEPS - 3)
-        def _():
-            one(c + 3).start()
-
-        pass_on(rows_at(c * CHUNK, CHUNK))
+        @pl.when(c < STEPS - AHEAD)
+        def _():
+            one(c + AHEAD).start()
+
+        pass_on(c)
         two(c).start()
         rest(c)
 
     to_ref[...] = jnp.broadcast_to(to[0:1, 15 * CHUNK :], to_ref.shape)
-    two(STEPS - 1).wait_recv()
+    rotated(7, 8)
     last_ref[...] = dot(late[15 * CHUNK :, :], r2[...]).astype(BF16)
 
     for name in f:
@@ -415,19 +420,26 @@
     for n in range(N_SECOND):
         s[n].wait_send()
     ranks.wait_send()
-    for half_chunk in (*one_halves, *two_halves):
-        half_chunk.wait_send()
-    for c in range(1, STEPS):
+    for c in range(STEPS):
         one(c).wait_send()
         two(c).wait_send()
 
 
-def finish(acc, last, to, out_ref):
-    start = pl.program_id(0) * TAIL
-    hot = ones_where(to[0:1, :] == iota((TAIL, CHUNK), 0) + start.astype(F32))
-    new = dot(hot.astype(BF16), last[...])
-    old = acc[rows_at(start, TAIL), :].astype(F32)
-    out_ref[...] = (old + new).astype(BF16)
+def finish(acc, last, to, out_hbm, out, sem):
+    def stored(t):
+        at = rows_at(t * TAIL, TAIL)
+        return pltpu.make_async_copy(out.at[at], out_hbm.at[at], sem.at[t])
+
+    @pl.loop(0, ROWS // TAIL)
+    def _(t):
+        at = rows_at(t * TAIL, TAIL)
+        hit = to[0:1, :] == iota((TAIL, CHUNK), 0) + (t * TAIL).astype(F32)
+        new = dot(ones_where(hit).astype(BF16), last[...])
+        out[at, :] = (acc[at, :].astype(F32) + new).astype(BF16)
+        stored(t).start()
+
+    for t in range(ROWS // TAIL):
+        stored(t).wait()
 
 
 def on_device(corpus, rotation_first, rotation_second, cross_first, cross_second):
@@ -485,10 +497,13 @@
     )
     return pl.pallas_call(
         finish,
-        grid=(ROWS // TAIL,),
         out_shape=jax.ShapeDtypeStruct((ROWS, D), BF16),
         in_specs=[vmem] * 3,
-        out_specs=pl.BlockSpec((TAIL, D), lambda t: (t, 0)),
+        out_specs=hbm,
+        scratch_shapes=[
+            pltpu.VMEM((ROWS, D), BF16),
+            pltpu.SemaphoreType.DMA((ROWS // TAIL,)),
+        ],
         compiler_params=pltpu.CompilerParams(vmem_limit_bytes=12 << 20),
         cost_estimate=pl.CostEstimate(
             flops=600_000_000, bytes_accessed=8 << 20, transcendentals=0

time: 94.1 us -> 89.6 us (0.952)
  Pallas kernels: 90.6 us -> 85.8 us
    pallas_call x1, Pallas kernels: 86 us -> 82.7 us  [on_device(): pl.pallas_call(kernel, out_shape=(jax.ShapeDtypeStruct((ROWS, D), BF16),...]
    pallas_call x1, Pallas kernels: 4.63 us -> 3.15 us  [on_device(): pl.pallas_call(finish, out_shape=jax.ShapeDtypeStruct((ROWS, D), BF16), i...]
where the time goes in v3:
time: 89.6 us; the launch traced here: 89.2 us
  Pallas kernels  85.8 us (96%)
  local copies, waits for them, and re-layouts  3.23 us (4%)
    pallas_call x1, Pallas kernels, on_device(): pl.pallas_call(kernel, out_shape=(jax.ShapeDtypeStruct((ROWS, D), BF16),...  82.7 us
    unnamed x8, local copies, waits for them, and re-layouts  3.23 us
    pallas_call x1, Pallas kernels, on_device(): pl.pallas_call(finish, out_shape=jax.ShapeDtypeStruct((ROWS, D), BF16), i...  3.15 us

profile of v3, /device:TPU:0, one launch (start us, length us, event | category | flops | bytes accessed | tf_op | source)
XLA Modules:
  0.0 89.2 jit_solution(15954085031069572242)
XLA Ops:
  0.0 0.0 copy-start
  0.0 0.9 %copy-done = bf16[1,128,1024]{2,1,0:T(8,128)(2,1)S(1)} copy-done((bf16[1,128,1024]{2,1,0:T(8,128)(2,1)S(1)}, bf16[1,128,1024]{2,1,0:T(8,128)(2,1)}, u32[]{:S(2)}) %copy-start) | copy-done | bytes 262168
  1.0 0.0 copy-start.1
  1.0 0.9 %copy-done.1 = bf16[1,64,1024]{2,1,0:T(8,128)(2,1)S(1)} copy-done((bf16[1,64,1024]{2,1,0:T(8,128)(2,1)S(1)}, bf16[1,64,1024]{2,1,0:T(8,128)(2,1)}, u32[]{:S(2)}) %copy-start.1) | copy-done | bytes 131096
  1.9 0.0 copy-start.2
  1.9 0.7 copy-done.2
  2.5 0.0 copy-start.3
  2.5 0.7 copy-done.3
  3.2 82.7 %shard_map.55 = (bf16[2048,1024]{1,0:T(8,128)(2,1)S(1)}, bf16[128,1024]{1,0:T(8,128)(2,1)S(1)}, f32[8,128]{1,0:T(8,128)S(1)}) custom-call(bf16[2048,1024]{1,0:T(8,128)(2,1)} %x_hbm.1, bf16[1,128,1024]{2,1,0:T(8,128)(2,1)S(1)} %copy-done, bf16[1,64,1024]{2,1,0:T(8,128)(2,1)S(1)} %copy-done.1, s32[1,1,1024]{2,1,0:T(1,128)S(1)} %copy-done.2, ...), custom_call_target="tpu_custom_call" | custom-call | flops 35999997952 | bytes 16777216 | tf_op jit(solution)/shard_map/pallas_call | solution.py:448
  85.9 3.1 %shard_map.56 = bf16[2048,1024]{1,0:T(8,128)(2,1)} custom-call(bf16[2048,1024]{1,0:T(8,128)(2,1)S(1)} %get-tuple-element.8.acc, bf16[128,1024]{1,0:T(8,128)(2,1)S(1)} %get-tuple-element.9.last, f32[8,128]{1,0:T(8,128)S(1)} %get-tuple-element.10.to), custom_call_target="tpu_custom_call" | custom-call | flops 600000000 | bytes 8388608 | tf_op jit(solution)/shard_map/pallas_call | solution.py:498
Async XLA Ops:
  0.0 0.9 %copy-start = (bf16[1,128,1024]{2,1,0:T(8,128)(2,1)S(1)}, bf16[1,128,1024]{2,1,0:T(8,128)(2,1)}, u32[]{:S(2)}) copy-start(bf16[1,128,1024]{2,1,0:T(8,128)(2,1)} %r1_hbm.1) | copy-start | bytes 786436
  1.0 0.9 %copy-start.1 = (bf16[1,64,1024]{2,1,0:T(8,128)(2,1)S(1)}, bf16[1,64,1024]{2,1,0:T(8,128)(2,1)}, u32[]{:S(2)}) copy-start(bf16[1,64,1024]{2,1,0:T(8,128)(2,1)} %r2_hbm.1) | copy-start | bytes 393220
  1.9 0.7 copy-start.2
  2.5 0.7 copy-start.3

commit v4 on v3

--- a/solution.py
+++ b/solution.py
@@ -17,7 +17,7 @@
 AHEAD = 3
 FIRST = 128
 SECOND = 64
-N_FIRST, N_SECOND = 15, 15
+N_FIRST, N_SECOND = 14, 15
 BLOCK = 512
 VMEM = 48 << 20
 TAIL = 256
@@ -141,8 +141,7 @@
         "up_near": first(10, pz, 1 - py, high, 64, z_up),
         "down_near": first(11, pz, 1 - py, high, 64, z_down),
         "near_far": first(12, on_z(2), py, low, 64, y_near),
-        "up_near_2": first(13, on_z(-1), 1 - py, high, 32, z_up),
-        "down_near_2": first(14, on_z(1), 1 - py, high + 32, 32, z_down),
+        "near_far_high": first(13, on_z(2), py, high, 64, y_near),
     }
 
     def forward(came, *names):
@@ -271,12 +270,8 @@
     pick(col1, sent1, 0)
     pl.loop(0, 1)(lambda b: pick(colg, raw2, b))
     forward("up_low_2", "near_far")
-    forward("up_near", "up_near_2")
-    forward("down_near", "down_near_2")
-    s[0].wait_recv()
-    for n in range(8, 15):
-        s[n].start()
-    for name in ("up_high", "down_high_2", "up_near_2", "down_near_2"):
+    forward("down_high_2", "near_far_high")
+    for name in ("up_high", "up_near", "down_near"):
         f[name].wait_recv()
     for c in range(2):
         one(c).start()
@@ -287,8 +282,12 @@
     find_first()
 
     loads[3].wait()
-    for name in ("near_low", "near_up", "near_down", "near_far"):
+    for name in ("near_low", "near_up", "near_down", "near_far", "near_far_high"):
         f[name].wait_recv()
+
+    s[0].wait_recv()
+    for n in range(8, 15):
+        s[n].start()
 
     def prepare(b):
         at = rows_at(b * 256, 256)

time: 89.6 us -> 85.4 us (0.953)
  Pallas kernels: 85.8 us -> 81.8 us
    pallas_call x1, Pallas kernels: 82.7 us -> 78.7 us  [on_device(): pl.pallas_call(kernel, out_shape=(jax.ShapeDtypeStruct((ROWS, D), BF16),...]
where the time goes in v4:
time: 85.4 us; the launch traced here: 85.2 us
  Pallas kernels  81.8 us (96%)
  local copies, waits for them, and re-layouts  3.23 us (4%)
    pallas_call x1, Pallas kernels, on_device(): pl.pallas_call(kernel, out_shape=(jax.ShapeDtypeStruct((ROWS, D), BF16),...  78.7 us
    unnamed x8, local copies, waits for them, and re-layouts  3.23 us
    pallas_call x1, Pallas kernels, on_device(): pl.pallas_call(finish, out_shape=jax.ShapeDtypeStruct((ROWS, D), BF16), i...  3.15 us

profile of v4, /device:TPU:0, one launch (start us, length us, event | category | flops | bytes accessed | tf_op | source)
XLA Modules:
  0.0 85.2 jit_solution(11976656248947109136)
XLA Ops:
  0.0 0.0 copy-start
  0.0 0.9 %copy-done = bf16[1,128,1024]{2,1,0:T(8,128)(2,1)S(1)} copy-done((bf16[1,128,1024]{2,1,0:T(8,128)(2,1)S(1)}, bf16[1,128,1024]{2,1,0:T(8,128)(2,1)}, u32[]{:S(2)}) %copy-start) | copy-done | bytes 262168
  1.0 0.0 copy-start.1
  1.0 0.9 %copy-done.1 = bf16[1,64,1024]{2,1,0:T(8,128)(2,1)S(1)} copy-done((bf16[1,64,1024]{2,1,0:T(8,128)(2,1)S(1)}, bf16[1,64,1024]{2,1,0:T(8,128)(2,1)}, u32[]{:S(2)}) %copy-start.1) | copy-done | bytes 131096
  1.9 0.0 copy-start.2
  1.9 0.7 copy-done.2
  2.5 0.0 copy-start.3
  2.5 0.7 copy-done.3
  3.2 78.7 %shard_map.55 = (bf16[2048,1024]{1,0:T(8,128)(2,1)S(1)}, bf16[128,1024]{1,0:T(8,128)(2,1)S(1)}, f32[8,128]{1,0:T(8,128)S(1)}) custom-call(bf16[2048,1024]{1,0:T(8,128)(2,1)} %x_hbm.1, bf16[1,128,1024]{2,1,0:T(8,128)(2,1)S(1)} %copy-done, bf16[1,64,1024]{2,1,0:T(8,128)(2,1)S(1)} %copy-done.1, s32[1,1,1024]{2,1,0:T(1,128)S(1)} %copy-done.2, ...), custom_call_target="tpu_custom_call" | custom-call | flops 35999997952 | bytes 16777216 | tf_op jit(solution)/shard_map/pallas_call | solution.py:447
  81.9 3.2 %shard_map.56 = bf16[2048,1024]{1,0:T(8,128)(2,1)} custom-call(bf16[2048,1024]{1,0:T(8,128)(2,1)S(1)} %get-tuple-element.8.acc, bf16[128,1024]{1,0:T(8,128)(2,1)S(1)} %get-tuple-element.9.last, f32[8,128]{1,0:T(8,128)S(1)} %get-tuple-element.10.to), custom_call_target="tpu_custom_call" | custom-call | flops 600000000 | bytes 8388608 | tf_op jit(solution)/shard_map/pallas_call | solution.py:497
Async XLA Ops:
  0.0 0.9 %copy-start = (bf16[1,128,1024]{2,1,0:T(8,128)(2,1)S(1)}, bf16[1,128,1024]{2,1,0:T(8,128)(2,1)}, u32[]{:S(2)}) copy-start(bf16[1,128,1024]{2,1,0:T(8,128)(2,1)} %r1_hbm.1) | copy-start | bytes 786436
  1.0 0.9 %copy-start.1 = (bf16[1,64,1024]{2,1,0:T(8,128)(2,1)S(1)}, bf16[1,64,1024]{2,1,0:T(8,128)(2,1)}, u32[]{:S(2)}) copy-start(bf16[1,64,1024]{2,1,0:T(8,128)(2,1)} %r2_hbm.1) | copy-start | bytes 393220
  1.9 0.7 copy-start.2
  2.5 0.7 copy-start.3

commit v5 on v4

--- a/solution.py
+++ b/solution.py
@@ -20,7 +20,7 @@
 N_FIRST, N_SECOND = 14, 15
 BLOCK = 512
 VMEM = 48 << 20
-TAIL = 256
+TAIL = 512
 
 AT_SECOND = N_FIRST
 AT_ONE = AT_SECOND + N_SECOND

time: 85.4 us -> 85 us (level)
  no operation moved by 1% of the time
where the time goes in v5:
time: 85 us; the launch traced here: 84.8 us
  Pallas kernels  81.4 us (96%)
  local copies, waits for them, and re-layouts  3.23 us (4%)
    pallas_call x1, Pallas kernels, on_device(): pl.pallas_call(kernel, out_shape=(jax.ShapeDtypeStruct((ROWS, D), BF16),...  78.7 us
    unnamed x8, local copies, waits for them, and re-layouts  3.23 us
    pallas_call x1, Pallas kernels, on_device(): pl.pallas_call(finish, out_shape=jax.ShapeDtypeStruct((ROWS, D), BF16), i...  2.69 us

profile of v5, /device:TPU:0, one launch (start us, length us, event | category | flops | bytes accessed | tf_op | source)
XLA Modules:
  0.0 84.8 jit_solution(2336669922489995579)
XLA Ops:
  0.0 0.0 copy-start
  0.0 0.9 %copy-done = bf16[1,128,1024]{2,1,0:T(8,128)(2,1)S(1)} copy-done((bf16[1,128,1024]{2,1,0:T(8,128)(2,1)S(1)}, bf16[1,128,1024]{2,1,0:T(8,128)(2,1)}, u32[]{:S(2)}) %copy-start) | copy-done | bytes 262168
  1.0 0.0 copy-start.1
  1.0 0.9 %copy-done.1 = bf16[1,64,1024]{2,1,0:T(8,128)(2,1)S(1)} copy-done((bf16[1,64,1024]{2,1,0:T(8,128)(2,1)S(1)}, bf16[1,64,1024]{2,1,0:T(8,128)(2,1)}, u32[]{:S(2)}) %copy-start.1) | copy-done | bytes 131096
  1.9 0.0 copy-start.2
  1.9 0.7 copy-done.2
  2.5 0.0 copy-start.3
  2.5 0.7 copy-done.3
  3.2 78.7 %shard_map.55 = (bf16[2048,1024]{1,0:T(8,128)(2,1)S(1)}, bf16[128,1024]{1,0:T(8,128)(2,1)S(1)}, f32[8,128]{1,0:T(8,128)S(1)}) custom-call(bf16[2048,1024]{1,0:T(8,128)(2,1)} %x_hbm.1, bf16[1,128,1024]{2,1,0:T(8,128)(2,1)S(1)} %copy-done, bf16[1,64,1024]{2,1,0:T(8,128)(2,1)S(1)} %copy-done.1, s32[1,1,1024]{2,1,0:T(1,128)S(1)} %copy-done.2, ...), custom_call_target="tpu_custom_call" | custom-call | flops 35999997952 | bytes 16777216 | tf_op jit(solution)/shard_map/pallas_call | solution.py:447
  81.9 2.7 %shard_map.56 = bf16[2048,1024]{1,0:T(8,128)(2,1)} custom-call(bf16[2048,1024]{1,0:T(8,128)(2,1)S(1)} %get-tuple-element.8.acc, bf16[128,1024]{1,0:T(8,128)(2,1)S(1)} %get-tuple-element.9.last, f32[8,128]{1,0:T(8,128)S(1)} %get-tuple-element.10.to), custom_call_target="tpu_custom_call" | custom-call | flops 600000000 | bytes 8388608 | tf_op jit(solution)/shard_map/pallas_call | solution.py:497
Async XLA Ops:
  0.0 0.9 %copy-start = (bf16[1,128,1024]{2,1,0:T(8,128)(2,1)S(1)}, bf16[1,128,1024]{2,1,0:T(8,128)(2,1)}, u32[]{:S(2)}) copy-start(bf16[1,128,1024]{2,1,0:T(8,128)(2,1)} %r1_hbm.1) | copy-start | bytes 786436
  1.0 0.9 %copy-start.1 = (bf16[1,64,1024]{2,1,0:T(8,128)(2,1)S(1)}, bf16[1,64,1024]{2,1,0:T(8,128)(2,1)}, u32[]{:S(2)}) copy-start(bf16[1,64,1024]{2,1,0:T(8,128)(2,1)} %r2_hbm.1) | copy-start | bytes 393220
  1.9 0.7 copy-start.2
  2.5 0.7 copy-start.3
